TPU v7x, 32 devices: a whole 2x2x4 slice. The times are simulated.
32 devices in a mesh: group: 2 (over core), kvh: 4 (over z), blk: 4 (over y, x).
Axes of the slice: x: 2, y: 2, z: 4, core: 2. Of those that a mesh axis runs over, the one named last changes fastest.
Arguments:
- resp_q: bfloat16 [1024, 64, 128], P(('group', 'blk'), 'kvh'), parts along dimension 0, may hold values from -8 to 8
- prompt_k: bfloat16 [2048, 8, 128], P(('group', 'blk'), 'kvh'), parts along dimension 0, may hold values from -8 to 8
- prompt_v: bfloat16 [2048, 8, 128], P(('group', 'blk'), 'kvh'), parts along dimension 0, may hold values from -6 to 6
- resp_k: bfloat16 [1024, 8, 128], P(('group', 'blk'), 'kvh'), parts along dimension 0, may hold values from -6 to 6
- resp_v: bfloat16 [1024, 8, 128], P(('group', 'blk'), 'kvh'), parts along dimension 0, may hold values from -6 to 6
- d_out: bfloat16 [1024, 64, 128], P(('group', 'blk'), 'kvh'), parts along dimension 0, may hold values from -6 to 6
- segment_ids: int32 [8, 128], P(('group', 'blk')), parts along dimension 0, may hold values from 0 to 3, never falling along the last dimension, each value on 1 to 64 neighbouring positions
- live_rows: int32 [8], P(('group', 'blk')), parts along dimension 0, may hold values from 1 to 128, 320 in all
Outputs:
- out: bfloat16 [1024, 64, 128], P(('group', 'blk'), 'kvh'), parts along dimension 0
- d_q: bfloat16 [1024, 64, 128], P(('group', 'blk'), 'kvh'), parts along dimension 0
- d_resp_k: bfloat16 [1024, 8, 128], P(('group', 'blk'), 'kvh'), parts along dimension 0
- d_resp_v: bfloat16 [1024, 8, 128], P(('group', 'blk'), 'kvh'), parts along dimension 0
- d_prompt_k: bfloat16 [2048, 8, 128], P(('group', 'blk'), 'kvh'), parts along dimension 0
- d_prompt_v: bfloat16 [2048, 8, 128], P(('group', 'blk'), 'kvh'), parts along dimension 0
There are 2 independent parts, one for each index of `group`. A program takes and returns all parts, laid end to end along the dimension named above; each array names one. Nothing has to cross between parts.
Inputs may be any that keep to these rules, and one draw needn't show every extreme that they name: `segment_ids`: within a device's rows the numbers never fall; one response holds at most 64 rows of a device, and some response reaches that. `live_rows`: rows of a device from this count on are padding; some device has all 128 rows live.
All inputs are finite; a program needn't handle non-finite values.
Results may differ from a plain program's by a relative error of at most 0.017.
Values may be sent and summed in bfloat16 or wider, within the bound.
A program may use at most 64 MiB of HBM per device.

v0:
```python
import math

import jax
import jax.numpy as jnp
from jax import lax
from jax.sharding import PartitionSpec as P


def from_behind(block, axis, distance):
    devices = range(lax.axis_size(axis))
    route = [((i - distance) % len(devices), i) for i in devices]
    return lax.ppermute(block, axis, route)


def on_device(resp_q, prompt_k, prompt_v, resp_k, resp_v, d_out, segment_ids, live_rows):
    q_rows, q_heads, head_dim = resp_q.shape
    kv_heads = resp_k.shape[1]
    grouped = resp_q.reshape(q_rows, kv_heads, q_heads // kv_heads, head_dim)
    factor = 1.0 / math.sqrt(head_dim)
    position = jnp.arange(q_rows)
    live_mask = (position < live_rows[0]).astype(jnp.bfloat16)
    out_grad = (d_out * live_mask[:, None, None]).reshape(grouped.shape)
    segment = segment_ids[0]
    local_mask = (position[None, :] <= position[:, None]) & (segment[:, None] == segment[None, :])

    def scores_for(key_block):
        return (
            jnp.einsum("rkgd,pkd->kgrp", grouped, key_block, preferred_element_type=jnp.float32)
            * factor
        )

    local_scores = jnp.where(local_mask, scores_for(resp_k), -jnp.inf)
    start_high = jnp.max(local_scores, axis=-1)
    start_total = jnp.sum(jnp.exp(local_scores - start_high[..., None]), axis=-1)
    block_keys = lax.all_gather(prompt_k, "blk", axis=0, tiled=True)
    block_width = math.gcd(block_keys.shape[0], 512)

    def stats_per_block(number, loop_state):
        highest, exp_total = loop_state
        keys_now = lax.dynamic_slice_in_dim(block_keys, number * block_width, block_width, 0)
        scores = scores_for(keys_now)
        new_high = jnp.maximum(highest, jnp.max(scores, axis=-1))
        exp_total = exp_total * jnp.exp(highest - new_high) + jnp.sum(
            jnp.exp(scores - new_high[..., None]), axis=-1
        )
        return (new_high, exp_total)

    highest, exp_total = lax.fori_loop(
        0, block_keys.shape[0] // block_width, stats_per_block, (start_high, start_total)
    )
    log_total = highest + jnp.log(exp_total)

    def weights_for(key_block):
        return jnp.exp(scores_for(key_block) - log_total[..., None])

    local_full = jnp.exp(local_scores - log_total[..., None])
    local_accum = jnp.einsum(
        "kgrp,pkd->rkgd",
        local_full.astype(jnp.bfloat16),
        resp_v,
        preferred_element_type=jnp.float32,
    )
    value_block_keys = lax.all_gather(prompt_k, "blk", axis=0, tiled=True)
    block_values = lax.all_gather(prompt_v, "blk", axis=0, tiled=True)
    value_block_width = math.gcd(value_block_keys.shape[0], 512)

    def value_per_block(number, accum):
        first_row = number * value_block_width
        keys_now = lax.dynamic_slice_in_dim(value_block_keys, first_row, value_block_width, 0)
        values_now = lax.dynamic_slice_in_dim(block_values, first_row, value_block_width, 0)
        weights_low = weights_for(keys_now).astype(jnp.bfloat16)
        return accum + jnp.einsum(
            "kgrp,pkd->rkgd", weights_low, values_now, preferred_element_type=jnp.float32
        )

    accum = lax.fori_loop(
        0, value_block_keys.shape[0] // value_block_width, value_per_block, local_accum
    )
    out_low = (accum * live_mask.astype(jnp.float32)[:, None, None, None]).astype(jnp.bfloat16)
    row_delta = jnp.transpose(
        jnp.sum(out_grad.astype(jnp.float32) * out_low.astype(jnp.float32), axis=-1), (1, 2, 0)
    )

    def back_terms(key_block, value_block, full_weights):
        weights_low = full_weights.astype(jnp.bfloat16)
        dprob = jnp.einsum(
            "rkgd,pkd->kgrp", out_grad, value_block, preferred_element_type=jnp.float32
        )
        dscore = (full_weights * (dprob - row_delta[..., None]) * factor).astype(jnp.bfloat16)
        query_part = jnp.einsum(
            "kgrp,pkd->rkgd", dscore, key_block, preferred_element_type=jnp.float32
        )
        key_part = jnp.einsum("kgrp,rkgd->pkd", dscore, grouped, preferred_element_type=jnp.float32)
        value_part = jnp.einsum(
            "kgrp,rkgd->pkd", weights_low, out_grad, preferred_element_type=jnp.float32
        )
        return (query_part, key_part, value_part)

    def prompt_terms(key_rows, value_rows, query_start):
        block_width = math.gcd(key_rows.shape[0], 512)

        def prompt_per_block(number, loop_state):
            query_accum, key_grads, value_grads = loop_state
            first_row = number * block_width
            query_part, key_part, value_part = back_terms(
                key_rows, value_rows, weights_for(key_rows)
            )
            key_grads = key_part
            value_grads = value_part
            return (query_accum + query_part, key_grads, value_grads)

        zero_rows = jnp.zeros(key_rows.shape, jnp.float32)
        return lax.fori_loop(
            0,
            key_rows.shape[0] // block_width,
            prompt_per_block,
            (query_start, zero_rows, zero_rows),
        )

    query_local, d_resp_k, d_resp_v = back_terms(resp_k, resp_v, local_full)
    devices = lax.axis_size("blk")

    def one_turn(number, loop_state):
        keys_now, values_now, key_accum, value_accum, query_accum = loop_state
        query_accum, key_part, value_part = prompt_terms(keys_now, values_now, query_accum)
        keys_now, values_now = from_behind((keys_now, values_now), "blk", 1)
        key_accum, value_accum = from_behind(
            (key_accum + key_part, value_accum + value_part), "blk", 1
        )
        return (keys_now, values_now, key_accum, value_accum, query_accum)

    zero_grad = jnp.zeros(prompt_k.shape, jnp.float32)
    final_state = lax.fori_loop(
        0, devices, one_turn, (prompt_k, prompt_v, zero_grad, zero_grad, query_local)
    )
    query_total = final_state[4]
    prompt_kgrad = final_state[2]
    prompt_vgrad = final_state[3]
    out = out_low.reshape(q_rows, q_heads, head_dim)
    d_q = query_total.astype(jnp.bfloat16).reshape(q_rows, q_heads, head_dim)
    return (
        out,
        d_q,
        d_resp_k.astype(jnp.bfloat16),
        d_resp_v.astype(jnp.bfloat16),
        prompt_kgrad.astype(jnp.bfloat16),
        prompt_vgrad.astype(jnp.bfloat16),
    )


def solution(mesh):
    return jax.shard_map(
        on_device,
        mesh=mesh,
        in_specs=(
            P(("group", "blk"), "kvh", None),
            P(("group", "blk"), "kvh", None),
            P(("group", "blk"), "kvh", None),
            P(("group", "blk"), "kvh", None),
            P(("group", "blk"), "kvh", None),
            P(("group", "blk"), "kvh", None),
            P(("group", "blk"), None),
            P(("group", "blk")),
        ),
        out_specs=(
            P(("group", "blk"), "kvh", None),
            P(("group", "blk"), "kvh", None),
            P(("group", "blk"), "kvh", None),
            P(("group", "blk"), "kvh", None),
            P(("group", "blk"), "kvh", None),
            P(("group", "blk"), "kvh", None),
        ),
        check_vma=False,
    )
```

profile of v0, /device:TPU:0, one launch (start us, length us, event | category | flops | bytes accessed | tf_op | source)
XLA Modules:
  0.0 136.3 jit_solution(5011705102718807547)
XLA Ops:
  1.9 1.2 broadcast_multiply_fusion
  4.2 11.5 %all_gather.7 = bf16[1024,2,128]{2,1,0:T(2,128)(2,1)S(1)} all-gather(bf16[256,2,128]{2,1,0:T(2,128)(2,1)S(1)} %copy-done.4), channel_id=1, replica_groups=mesh['group'=2,'kvh'=4,'blk'=4] {'blk'}, dimensions={0}, use_global_device_ids=true | all-gather | bytes 655360 | tf_op jit(solution)/shard_map/all_gather | solution.py:35
  15.7 3.4 %while.52 = (s32[]{:T(128)}, f32[2,8,128]{2,1,0:T(8,128)S(1)}, f32[2,8,128]{2,1,0:T(8,128)S(1)}, bf16[1024,2,128]{2,1,0:T(2,128)(2,1)S(1)}, bf16[128,2,8,128]{3,...) while((s32[]{:T(128)}, f32[2,8,128]{2,1,0:T(8,128)S(1)}, ...), condition=%wide.region_5.6_spmd, body=%wide.region_2.5_spmd.sunk | while | flops 273682432 | bytes 9805975 | solution.py:48
  19.1 1.4 %convolution_bitcast_fusion.5 = f32[128,2,8,128]{3,0,2,1:T(8,128)} fusion(f32[2,8,128,128]{2,3,1,0:T(8,128)S(1)} %get-tuple-element.399, f32[2,8,128]{2,1,0:T(8,128)S(1)} %log_add_fusion, bf16[128,2,128,1]{2,1,0,3:T(2,128)(2,1)S(1)} %bitcast.197), kind=kOutput, calls=%fused_computation.43 | convolution fusion | flops 67633152 | bytes 2170880 | tf_op jit(solution)/shard_map/kgrp,pkd->rkgd/dot_general | solution.py:57
  20.5 2.5 %copy.46 = f32[128,2,8,128]{0,3,2,1:T(8,128)} copy(f32[128,2,8,128]{3,0,2,1:T(8,128)} %convolution_bitcast_fusion.5) | data formatting | bytes 2097152 | tf_op jit(solution)/shard_map/while | solution.py:76
  23.2 12.1 %all_gather.8 = bf16[1024,2,128]{0,2,1:T(8,128)(2,1)S(1)} all-gather(bf16[256,2,128]{0,2,1:T(8,128)(2,1)S(1)} %copy.45), channel_id=1, replica_groups=mesh['group'=2,'kvh'=4,'blk'=4] {'blk'}, dimensions={0}, use_global_device_ids=true | all-gather | bytes 655360 | tf_op jit(solution)/shard_map/all_gather | solution.py:64
  35.3 8.3 %while.53 = (s32[]{:T(128)}, f32[128,2,8,128]{0,3,2,1:T(8,128)}, bf16[1024,2,128]{0,2,1:T(8,128)(2,1)S(1)}, bf16[1024,2,128]{2,1,0:T(2,128)(2,1)S(1)}, bf16[128,...) while((s32[]{:T(128)}, f32[128,2,8,128]{0,3,2,1:T(8,128)}, ...), condition=%wide.region_7.8_spmd, body=%wide.region_6.7_spmd.sunk | while | flops 540278784 | bytes 3678371 | solution.py:76
  35.5 3.9 %fusion.92 = f32[128,2,8,128]{0,3,2,1:T(8,128)} fusion(f32[128,2,8,128]{0,3,2,1:T(8,128)} %get-tuple-element.573, f32[2,8,128]{2,1,0:T(8,128)S(1)} %get-tuple-element.587, bf16[128,2,8,128]{3,2,1,0:T(8,128)(2,1)} %get-tuple-element.586, bf16[512,2,128,1]{2,1,0,3:T(2,128)(2,1)S(1)} %dynamic-slice_bitcast_fusion.2, ...), kind=kOutput, calls=%fused_computation.13.clone.1 | convolution fusion | flops 540278784 | bytes 3153924 | tf_op jit(solution)/shard_map/while/body/eval_jaxpr/kgrp,pkd->rkgd/dot_general | solution.py:72
  39.6 3.9 %fusion.92 = f32[128,2,8,128]{0,3,2,1:T(8,128)} fusion(f32[128,2,8,128]{0,3,2,1:T(8,128)} %get-tuple-element.573, f32[2,8,128]{2,1,0:T(8,128)S(1)} %get-tuple-element.587, bf16[128,2,8,128]{3,2,1,0:T(8,128)(2,1)} %get-tuple-element.586, bf16[512,2,128,1]{2,1,0,3:T(2,128)(2,1)S(1)} %dynamic-slice_bitcast_fusion.2, ...), kind=kOutput, calls=%fused_computation.13.clone.1 | convolution fusion | flops 540278784 | bytes 3153924 | tf_op jit(solution)/shard_map/while/body/eval_jaxpr/kgrp,pkd->rkgd/dot_general | solution.py:72
  43.5 1.6 %copy.48 = f32[128,2,8,128]{3,0,2,1:T(8,128)S(1)} copy(f32[128,2,8,128]{0,3,2,1:T(8,128)} %get-tuple-element.294) | data formatting | bytes 2097152 | tf_op jit(solution)/shard_map/while | solution.py:76
  45.6 1.1 copy.125
  51.1 78.1 %while.54 = (s32[]{:T(128)}, bf16[256,2,128]{2,0,1:T(8,128)(2,1)}, bf16[256,2,128]{2,0,1:T(8,128)(2,1)}, f32[256,2,128]{2,0,1:T(8,128)}, f32[256,2,128]{2,0,1:T(...) while((s32[]{:T(128)}, bf16[256,2,128]{2,0,1:T(8,128)(2,1)}, ...), condition=%wide.region_10.0_spmd, body=%wide.region_9.10_spmd.sunk | while | flops 676200448 | bytes 18768140 | solution.py:133
  51.1 0.9 copy.154
  52.5 0.9 copy.155
  53.4 1.5 %collective-permute-start.1 = (bf16[256,2,128]{2,0,1:T(8,128)(2,1)S(1)}, bf16[256,2,128]{2,0,1:T(8,128)(2,1)}, u32[]{:S(2)}, u32[]{:S(2)}) collective-permute-start(bf16[256,2,128]{2,0,1:T(8,128)(2,1)S(1)} %copy.155), channel_id=1, source_target_pairs={{3,0},{0,1},{1,2},{2,3},{7,4},{4,5},{5,6},{6,7},{11,8},{8,9},{9,10... | collective-permute-start | bytes 393224 | tf_op jit(solution)/shard_map/while/body/eval_jaxpr/ppermute | solution.py:12
  56.0 2.1 %fusion.105 = f32[256,2,128]{2,0,1:T(8,128)} fusion(f32[256,2,128]{2,0,1:T(8,128)} %get-tuple-element.606, bf16[2,8,128,256]{2,3,1,0:T(8,128)(2,1)S(1)} %fusion.104, bf16[128,2,8,128]{3,0,2,1:T(8,128)(2,1)S(1)} %get-tuple-element.620), kind=kOutput, calls=%fused_computation.32.clone.1 | convolution fusion | flops 134283264 | bytes 2097152 | tf_op jit(solution)/shard_map/while/body/eval_jaxpr/while/body/eval_jaxpr/kgrp,rkgd->pkd/dot_general | solution.py:93
  58.1 1.5 %collective-permute-start.2 = (f32[256,2,128]{2,0,1:T(8,128)}, f32[256,2,128]{2,0,1:T(8,128)}, u32[]{:S(2)}, u32[]{:S(2)}) collective-permute-start(f32[256,2,128]{2,0,1:T(8,128)} %fusion.105), channel_id=1, source_target_pairs={{3,0},{0,1},{1,2},{2,3},{7,4},{4,5},{5,6},{6,7},{11,8},{8,9},{9,10... | collective-permute-start | bytes 786440 | tf_op jit(solution)/shard_map/while/body/eval_jaxpr/ppermute | solution.py:12
  59.6 2.2 %fusion.106 = f32[256,2,128]{2,0,1:T(8,128)} fusion(f32[256,2,128]{2,0,1:T(8,128)} %get-tuple-element.607, bf16[128,2,8,128]{3,0,2,1:T(8,128)(2,1)S(1)} %get-tuple-element.622, f32[2,256,128,8]{2,1,3,0:T(8,128)S(1)} %fusion.103, f32[2,8,128]{2,1,0:T(8,128)S(1)} %get-tuple-element.621), kind=kOutput, calls=%fused_computation.33.clone.1 | convolution fusion | flops 135856128 | bytes 3153920 | tf_op jit(solution)/shard_map/while/body/eval_jaxpr/while/body/eval_jaxpr/kgrp,rkgd->pkd/dot_general | solution.py:94
  61.8 1.5 %collective-permute-start.3 = (f32[256,2,128]{2,0,1:T(8,128)}, f32[256,2,128]{2,0,1:T(8,128)}, u32[]{:S(2)}, u32[]{:S(2)}) collective-permute-start(f32[256,2,128]{2,0,1:T(8,128)} %fusion.106), channel_id=1, source_target_pairs={{3,0},{0,1},{1,2},{2,3},{7,4},{4,5},{5,6},{6,7},{11,8},{8,9},{9,10... | collective-permute-start | bytes 786440 | tf_op jit(solution)/shard_map/while/body/eval_jaxpr/ppermute | solution.py:12
  63.9 3.8 %collective-permute-done.2 = f32[256,2,128]{2,0,1:T(8,128)} collective-permute-done((f32[256,2,128]{2,0,1:T(8,128)}, f32[256,2,128]{2,0,1:T(8,128)}, u32[]{:S(2)}, u32[]{:S(2)}) %collective-permute-start.2) | collective-permute-done | bytes 262176 | tf_op jit(solution)/shard_map/while/body/eval_jaxpr/ppermute | solution.py:12
  67.8 2.8 %collective-permute-done.3 = f32[256,2,128]{2,0,1:T(8,128)} collective-permute-done((f32[256,2,128]{2,0,1:T(8,128)}, f32[256,2,128]{2,0,1:T(8,128)}, u32[]{:S(2)}, u32[]{:S(2)}) %collective-permute-start.3) | collective-permute-done | bytes 262176 | tf_op jit(solution)/shard_map/while/body/eval_jaxpr/ppermute | solution.py:12
  70.6 0.9 copy.154
  71.5 0.9 copy.155
  72.4 2.1 %collective-permute-start.1 = (bf16[256,2,128]{2,0,1:T(8,128)(2,1)S(1)}, bf16[256,2,128]{2,0,1:T(8,128)(2,1)}, u32[]{:S(2)}, u32[]{:S(2)}) collective-permute-start(bf16[256,2,128]{2,0,1:T(8,128)(2,1)S(1)} %copy.155), channel_id=1, source_target_pairs={{3,0},{0,1},{1,2},{2,3},{7,4},{4,5},{5,6},{6,7},{11,8},{8,9},{9,10... | collective-permute-start | bytes 393224 | tf_op jit(solution)/shard_map/while/body/eval_jaxpr/ppermute | solution.py:12
  75.7 2.1 %fusion.105 = f32[256,2,128]{2,0,1:T(8,128)} fusion(f32[256,2,128]{2,0,1:T(8,128)} %get-tuple-element.606, bf16[2,8,128,256]{2,3,1,0:T(8,128)(2,1)S(1)} %fusion.104, bf16[128,2,8,128]{3,0,2,1:T(8,128)(2,1)S(1)} %get-tuple-element.620), kind=kOutput, calls=%fused_computation.32.clone.1 | convolution fusion | flops 134283264 | bytes 2097152 | tf_op jit(solution)/shard_map/while/body/eval_jaxpr/while/body/eval_jaxpr/kgrp,rkgd->pkd/dot_general | solution.py:93
  78.2 2.2 %fusion.106 = f32[256,2,128]{2,0,1:T(8,128)} fusion(f32[256,2,128]{2,0,1:T(8,128)} %get-tuple-element.607, bf16[128,2,8,128]{3,0,2,1:T(8,128)(2,1)S(1)} %get-tuple-element.622, f32[2,256,128,8]{2,1,3,0:T(8,128)S(1)} %fusion.103, f32[2,8,128]{2,1,0:T(8,128)S(1)} %get-tuple-element.621), kind=kOutput, calls=%fused_computation.33.clone.1 | convolution fusion | flops 135856128 | bytes 3153920 | tf_op jit(solution)/shard_map/while/body/eval_jaxpr/while/body/eval_jaxpr/kgrp,rkgd->pkd/dot_general | solution.py:94
  80.4 2.4 %collective-permute-start.3 = (f32[256,2,128]{2,0,1:T(8,128)}, f32[256,2,128]{2,0,1:T(8,128)}, u32[]{:S(2)}, u32[]{:S(2)}) collective-permute-start(f32[256,2,128]{2,0,1:T(8,128)} %fusion.106), channel_id=1, source_target_pairs={{3,0},{0,1},{1,2},{2,3},{7,4},{4,5},{5,6},{6,7},{11,8},{8,9},{9,10... | collective-permute-start | bytes 786440 | tf_op jit(solution)/shard_map/while/body/eval_jaxpr/ppermute | solution.py:12
  83.5 3.8 %collective-permute-done.2 = f32[256,2,128]{2,0,1:T(8,128)} collective-permute-done((f32[256,2,128]{2,0,1:T(8,128)}, f32[256,2,128]{2,0,1:T(8,128)}, u32[]{:S(2)}, u32[]{:S(2)}) %collective-permute-start.2) | collective-permute-done | bytes 262176 | tf_op jit(solution)/shard_map/while/body/eval_jaxpr/ppermute | solution.py:12
  87.3 2.8 %collective-permute-done.3 = f32[256,2,128]{2,0,1:T(8,128)} collective-permute-done((f32[256,2,128]{2,0,1:T(8,128)}, f32[256,2,128]{2,0,1:T(8,128)}, u32[]{:S(2)}, u32[]{:S(2)}) %collective-permute-start.3) | collective-permute-done | bytes 262176 | tf_op jit(solution)/shard_map/while/body/eval_jaxpr/ppermute | solution.py:12
  90.1 0.9 copy.154
  91.0 0.9 copy.155
  91.9 2.1 %collective-permute-start.1 = (bf16[256,2,128]{2,0,1:T(8,128)(2,1)S(1)}, bf16[256,2,128]{2,0,1:T(8,128)(2,1)}, u32[]{:S(2)}, u32[]{:S(2)}) collective-permute-start(bf16[256,2,128]{2,0,1:T(8,128)(2,1)S(1)} %copy.155), channel_id=1, source_target_pairs={{3,0},{0,1},{1,2},{2,3},{7,4},{4,5},{5,6},{6,7},{11,8},{8,9},{9,10... | collective-permute-start | bytes 393224 | tf_op jit(solution)/shard_map/while/body/eval_jaxpr/ppermute | solution.py:12
  95.2 2.1 %fusion.105 = f32[256,2,128]{2,0,1:T(8,128)} fusion(f32[256,2,128]{2,0,1:T(8,128)} %get-tuple-element.606, bf16[2,8,128,256]{2,3,1,0:T(8,128)(2,1)S(1)} %fusion.104, bf16[128,2,8,128]{3,0,2,1:T(8,128)(2,1)S(1)} %get-tuple-element.620), kind=kOutput, calls=%fused_computation.32.clone.1 | convolution fusion | flops 134283264 | bytes 2097152 | tf_op jit(solution)/shard_map/while/body/eval_jaxpr/while/body/eval_jaxpr/kgrp,rkgd->pkd/dot_general | solution.py:93
  97.4 2.2 %fusion.106 = f32[256,2,128]{2,0,1:T(8,128)} fusion(f32[256,2,128]{2,0,1:T(8,128)} %get-tuple-element.607, bf16[128,2,8,128]{3,0,2,1:T(8,128)(2,1)S(1)} %get-tuple-element.622, f32[2,256,128,8]{2,1,3,0:T(8,128)S(1)} %fusion.103, f32[2,8,128]{2,1,0:T(8,128)S(1)} %get-tuple-element.621), kind=kOutput, calls=%fused_computation.33.clone.1 | convolution fusion | flops 135856128 | bytes 3153920 | tf_op jit(solution)/shard_map/while/body/eval_jaxpr/while/body/eval_jaxpr/kgrp,rkgd->pkd/dot_general | solution.py:94
  99.6 2.7 %collective-permute-start.3 = (f32[256,2,128]{2,0,1:T(8,128)}, f32[256,2,128]{2,0,1:T(8,128)}, u32[]{:S(2)}, u32[]{:S(2)}) collective-permute-start(f32[256,2,128]{2,0,1:T(8,128)} %fusion.106), channel_id=1, source_target_pairs={{3,0},{0,1},{1,2},{2,3},{7,4},{4,5},{5,6},{6,7},{11,8},{8,9},{9,10... | collective-permute-start | bytes 786440 | tf_op jit(solution)/shard_map/while/body/eval_jaxpr/ppermute | solution.py:12
  103.0 3.8 %collective-permute-done.2 = f32[256,2,128]{2,0,1:T(8,128)} collective-permute-done((f32[256,2,128]{2,0,1:T(8,128)}, f32[256,2,128]{2,0,1:T(8,128)}, u32[]{:S(2)}, u32[]{:S(2)}) %collective-permute-start.2) | collective-permute-done | bytes 262176 | tf_op jit(solution)/shard_map/while/body/eval_jaxpr/ppermute | solution.py:12
  106.8 2.8 %collective-permute-done.3 = f32[256,2,128]{2,0,1:T(8,128)} collective-permute-done((f32[256,2,128]{2,0,1:T(8,128)}, f32[256,2,128]{2,0,1:T(8,128)}, u32[]{:S(2)}, u32[]{:S(2)}) %collective-permute-start.3) | collective-permute-done | bytes 262176 | tf_op jit(solution)/shard_map/while/body/eval_jaxpr/ppermute | solution.py:12
  109.6 0.9 copy.154
  110.5 0.9 copy.155
  111.4 2.1 %collective-permute-start.1 = (bf16[256,2,128]{2,0,1:T(8,128)(2,1)S(1)}, bf16[256,2,128]{2,0,1:T(8,128)(2,1)}, u32[]{:S(2)}, u32[]{:S(2)}) collective-permute-start(bf16[256,2,128]{2,0,1:T(8,128)(2,1)S(1)} %copy.155), channel_id=1, source_target_pairs={{3,0},{0,1},{1,2},{2,3},{7,4},{4,5},{5,6},{6,7},{11,8},{8,9},{9,10... | collective-permute-start | bytes 393224 | tf_op jit(solution)/shard_map/while/body/eval_jaxpr/ppermute | solution.py:12
  114.7 2.1 %fusion.105 = f32[256,2,128]{2,0,1:T(8,128)} fusion(f32[256,2,128]{2,0,1:T(8,128)} %get-tuple-element.606, bf16[2,8,128,256]{2,3,1,0:T(8,128)(2,1)S(1)} %fusion.104, bf16[128,2,8,128]{3,0,2,1:T(8,128)(2,1)S(1)} %get-tuple-element.620), kind=kOutput, calls=%fused_computation.32.clone.1 | convolution fusion | flops 134283264 | bytes 2097152 | tf_op jit(solution)/shard_map/while/body/eval_jaxpr/while/body/eval_jaxpr/kgrp,rkgd->pkd/dot_general | solution.py:93
  116.8 2.2 %fusion.106 = f32[256,2,128]{2,0,1:T(8,128)} fusion(f32[256,2,128]{2,0,1:T(8,128)} %get-tuple-element.607, bf16[128,2,8,128]{3,0,2,1:T(8,128)(2,1)S(1)} %get-tuple-element.622, f32[2,256,128,8]{2,1,3,0:T(8,128)S(1)} %fusion.103, f32[2,8,128]{2,1,0:T(8,128)S(1)} %get-tuple-element.621), kind=kOutput, calls=%fused_computation.33.clone.1 | convolution fusion | flops 135856128 | bytes 3153920 | tf_op jit(solution)/shard_map/while/body/eval_jaxpr/while/body/eval_jaxpr/kgrp,rkgd->pkd/dot_general | solution.py:94
  119.0 2.8 %collective-permute-start.3 = (f32[256,2,128]{2,0,1:T(8,128)}, f32[256,2,128]{2,0,1:T(8,128)}, u32[]{:S(2)}, u32[]{:S(2)}) collective-permute-start(f32[256,2,128]{2,0,1:T(8,128)} %fusion.106), channel_id=1, source_target_pairs={{3,0},{0,1},{1,2},{2,3},{7,4},{4,5},{5,6},{6,7},{11,8},{8,9},{9,10... | collective-permute-start | bytes 786440 | tf_op jit(solution)/shard_map/while/body/eval_jaxpr/ppermute | solution.py:12
  122.5 3.8 %collective-permute-done.2 = f32[256,2,128]{2,0,1:T(8,128)} collective-permute-done((f32[256,2,128]{2,0,1:T(8,128)}, f32[256,2,128]{2,0,1:T(8,128)}, u32[]{:S(2)}, u32[]{:S(2)}) %collective-permute-start.2) | collective-permute-done | bytes 262176 | tf_op jit(solution)/shard_map/while/body/eval_jaxpr/ppermute | solution.py:12
  126.3 2.8 %collective-permute-done.3 = f32[256,2,128]{2,0,1:T(8,128)} collective-permute-done((f32[256,2,128]{2,0,1:T(8,128)}, f32[256,2,128]{2,0,1:T(8,128)}, u32[]{:S(2)}, u32[]{:S(2)}) %collective-permute-start.3) | collective-permute-done | bytes 262176 | tf_op jit(solution)/shard_map/while/body/eval_jaxpr/ppermute | solution.py:12
  129.2 1.1 copy.124
  132.7 1.8 %copy.119 = bf16[256,2,128]{2,1,0:T(2,128)(2,1)} copy(f32[256,2,128]{2,0,1:T(8,128)} %get-tuple-element.296) | data formatting | bytes 393216 | tf_op jit(solution)/shard_map/while | solution.py:133
  134.5 1.8 %copy.118 = bf16[256,2,128]{2,1,0:T(2,128)(2,1)} copy(f32[256,2,128]{2,0,1:T(8,128)} %get-tuple-element.297) | data formatting | bytes 393216 | tf_op jit(solution)/shard_map/while | solution.py:133
  (90 shorter events, 20.9 us)
Async XLA Ops:
  0.6 18.5 %copy-start = (bf16[128,2,128]{2,1,0:T(2,128)(2,1)S(1)}, bf16[128,2,128]{2,1,0:T(2,128)(2,1)}, u32[]{:S(2)}) copy-start(bf16[128,2,128]{2,1,0:T(2,128)(2,1)} %param.18) | copy-start | bytes 196612
  0.6 2.7 %copy-start.6 = (bf16[128,16,128]{2,1,0:T(8,128)(2,1)S(1)}, bf16[128,16,128]{2,1,0:T(8,128)(2,1)}, u32[]{:S(2)}) copy-start(bf16[128,16,128]{2,1,0:T(8,128)(2,1)} %param.14) | copy-start | bytes 1572868
  0.7 2.9 %copy-start.9 = (bf16[128,2,128]{2,1,0:T(2,128)(2,1)S(1)}, bf16[128,2,128]{2,1,0:T(2,128)(2,1)}, u32[]{:S(2)}) copy-start(bf16[128,2,128]{2,1,0:T(2,128)(2,1)} %param.17) | copy-start | bytes 196612
  0.7 2.8 %copy-start.12 = (s32[1,128]{1,0:T(1,128)S(1)}, s32[1,128]{1,0:T(1,128)}, u32[]{:S(2)}) copy-start(s32[1,128]{1,0:T(1,128)} %param.20) | copy-start | bytes 1540
  1.9 2.0 %copy-start.10 = (bf16[128]{0:T(256)(128)(2,1)}, bf16[128]{0:T(256)(128)(2,1)S(1)}, u32[]{:S(2)}) copy-start(bf16[128]{0:T(256)(128)(2,1)S(1)} %get-tuple-element.400) | copy-start | bytes 772
  3.3 0.9 copy-start.4
  19.1 3.9 %copy-start.7 = (bf16[256,2,128]{2,1,0:T(2,128)(2,1)S(1)}, bf16[256,2,128]{2,1,0:T(2,128)(2,1)}, u32[]{:S(2)}) copy-start(bf16[256,2,128]{2,1,0:T(2,128)(2,1)} %param.16) | copy-start | bytes 393220
  43.5 1.6 %copy-start.13 = (f32[128]{0:T(128)S(1)}, f32[128]{0:T(128)}, u32[]{:S(2)}) copy-start(f32[128]{0:T(128)} %get-tuple-element.401) | copy-start | bytes 1540
  45.1 1.7 %copy-start.5 = (bf16[256,2,128]{2,1,0:T(2,128)(2,1)S(1)}, bf16[256,2,128]{2,1,0:T(2,128)(2,1)}, u32[]{:S(2)}) copy-start(bf16[256,2,128]{2,1,0:T(2,128)(2,1)} %param.15) | copy-start | bytes 393220
  45.1 2.3 %copy-start.8 = (bf16[256,2,128]{2,1,0:T(2,128)(2,1)S(1)}, bf16[256,2,128]{2,1,0:T(2,128)(2,1)}, u32[]{:S(2)}) copy-start(bf16[256,2,128]{2,1,0:T(2,128)(2,1)} %param.16) | copy-start | bytes 393220
  48.5 0.8 copy-start.1
  52.0 12.0 %collective-permute-start = (bf16[256,2,128]{2,0,1:T(8,128)(2,1)S(1)}, bf16[256,2,128]{2,0,1:T(8,128)(2,1)}, u32[]{:S(2)}, u32[]{:S(2)}) collective-permute-start(bf16[256,2,128]{2,0,1:T(8,128)(2,1)S(1)} %copy.154), channel_id=1, source_target_pairs={{3,0},{0,1},{1,2},{2,3},{7,4},{4,5},{5,6},{6,7},{11,8},{8,9},{9,10... | collective-permute-start | bytes 393224 | tf_op jit(solution)/shard_map/while/body/eval_jaxpr/ppermute | solution.py:12
  53.4 10.5 %collective-permute-start.1 = (bf16[256,2,128]{2,0,1:T(8,128)(2,1)S(1)}, bf16[256,2,128]{2,0,1:T(8,128)(2,1)}, u32[]{:S(2)}, u32[]{:S(2)}) collective-permute-start(bf16[256,2,128]{2,0,1:T(8,128)(2,1)S(1)} %copy.155), channel_id=1, source_target_pairs={{3,0},{0,1},{1,2},{2,3},{7,4},{4,5},{5,6},{6,7},{11,8},{8,9},{9,10... | collective-permute-start | bytes 393224 | tf_op jit(solution)/shard_map/while/body/eval_jaxpr/ppermute | solution.py:12
  58.1 9.7 %collective-permute-start.2 = (f32[256,2,128]{2,0,1:T(8,128)}, f32[256,2,128]{2,0,1:T(8,128)}, u32[]{:S(2)}, u32[]{:S(2)}) collective-permute-start(f32[256,2,128]{2,0,1:T(8,128)} %fusion.105), channel_id=1, source_target_pairs={{3,0},{0,1},{1,2},{2,3},{7,4},{4,5},{5,6},{6,7},{11,8},{8,9},{9,10... | collective-permute-start | bytes 786440 | tf_op jit(solution)/shard_map/while/body/eval_jaxpr/ppermute | solution.py:12
  61.8 8.8 %collective-permute-start.3 = (f32[256,2,128]{2,0,1:T(8,128)}, f32[256,2,128]{2,0,1:T(8,128)}, u32[]{:S(2)}, u32[]{:S(2)}) collective-permute-start(f32[256,2,128]{2,0,1:T(8,128)} %fusion.106), channel_id=1, source_target_pairs={{3,0},{0,1},{1,2},{2,3},{7,4},{4,5},{5,6},{6,7},{11,8},{8,9},{9,10... | collective-permute-start | bytes 786440 | tf_op jit(solution)/shard_map/while/body/eval_jaxpr/ppermute | solution.py:12
  71.5 12.0 %collective-permute-start = (bf16[256,2,128]{2,0,1:T(8,128)(2,1)S(1)}, bf16[256,2,128]{2,0,1:T(8,128)(2,1)}, u32[]{:S(2)}, u32[]{:S(2)}) collective-permute-start(bf16[256,2,128]{2,0,1:T(8,128)(2,1)S(1)} %copy.154), channel_id=1, source_target_pairs={{3,0},{0,1},{1,2},{2,3},{7,4},{4,5},{5,6},{6,7},{11,8},{8,9},{9,10... | collective-permute-start | bytes 393224 | tf_op jit(solution)/shard_map/while/body/eval_jaxpr/ppermute | solution.py:12
  72.4 11.1 %collective-permute-start.1 = (bf16[256,2,128]{2,0,1:T(8,128)(2,1)S(1)}, bf16[256,2,128]{2,0,1:T(8,128)(2,1)}, u32[]{:S(2)}, u32[]{:S(2)}) collective-permute-start(bf16[256,2,128]{2,0,1:T(8,128)(2,1)S(1)} %copy.155), channel_id=1, source_target_pairs={{3,0},{0,1},{1,2},{2,3},{7,4},{4,5},{5,6},{6,7},{11,8},{8,9},{9,10... | collective-permute-start | bytes 393224 | tf_op jit(solution)/shard_map/while/body/eval_jaxpr/ppermute | solution.py:12
  77.8 9.5 %collective-permute-start.2 = (f32[256,2,128]{2,0,1:T(8,128)}, f32[256,2,128]{2,0,1:T(8,128)}, u32[]{:S(2)}, u32[]{:S(2)}) collective-permute-start(f32[256,2,128]{2,0,1:T(8,128)} %fusion.105), channel_id=1, source_target_pairs={{3,0},{0,1},{1,2},{2,3},{7,4},{4,5},{5,6},{6,7},{11,8},{8,9},{9,10... | collective-permute-start | bytes 786440 | tf_op jit(solution)/shard_map/while/body/eval_jaxpr/ppermute | solution.py:12
  80.4 9.7 %collective-permute-start.3 = (f32[256,2,128]{2,0,1:T(8,128)}, f32[256,2,128]{2,0,1:T(8,128)}, u32[]{:S(2)}, u32[]{:S(2)}) collective-permute-start(f32[256,2,128]{2,0,1:T(8,128)} %fusion.106), channel_id=1, source_target_pairs={{3,0},{0,1},{1,2},{2,3},{7,4},{4,5},{5,6},{6,7},{11,8},{8,9},{9,10... | collective-permute-start | bytes 786440 | tf_op jit(solution)/shard_map/while/body/eval_jaxpr/ppermute | solution.py:12
  91.0 12.0 %collective-permute-start = (bf16[256,2,128]{2,0,1:T(8,128)(2,1)S(1)}, bf16[256,2,128]{2,0,1:T(8,128)(2,1)}, u32[]{:S(2)}, u32[]{:S(2)}) collective-permute-start(bf16[256,2,128]{2,0,1:T(8,128)(2,1)S(1)} %copy.154), channel_id=1, source_target_pairs={{3,0},{0,1},{1,2},{2,3},{7,4},{4,5},{5,6},{6,7},{11,8},{8,9},{9,10... | collective-permute-start | bytes 393224 | tf_op jit(solution)/shard_map/while/body/eval_jaxpr/ppermute | solution.py:12
  91.9 11.1 %collective-permute-start.1 = (bf16[256,2,128]{2,0,1:T(8,128)(2,1)S(1)}, bf16[256,2,128]{2,0,1:T(8,128)(2,1)}, u32[]{:S(2)}, u32[]{:S(2)}) collective-permute-start(bf16[256,2,128]{2,0,1:T(8,128)(2,1)S(1)} %copy.155), channel_id=1, source_target_pairs={{3,0},{0,1},{1,2},{2,3},{7,4},{4,5},{5,6},{6,7},{11,8},{8,9},{9,10... | collective-permute-start | bytes 393224 | tf_op jit(solution)/shard_map/while/body/eval_jaxpr/ppermute | solution.py:12
  97.3 9.5 %collective-permute-start.2 = (f32[256,2,128]{2,0,1:T(8,128)}, f32[256,2,128]{2,0,1:T(8,128)}, u32[]{:S(2)}, u32[]{:S(2)}) collective-permute-start(f32[256,2,128]{2,0,1:T(8,128)} %fusion.105), channel_id=1, source_target_pairs={{3,0},{0,1},{1,2},{2,3},{7,4},{4,5},{5,6},{6,7},{11,8},{8,9},{9,10... | collective-permute-start | bytes 786440 | tf_op jit(solution)/shard_map/while/body/eval_jaxpr/ppermute | solution.py:12
  99.6 10.0 %collective-permute-start.3 = (f32[256,2,128]{2,0,1:T(8,128)}, f32[256,2,128]{2,0,1:T(8,128)}, u32[]{:S(2)}, u32[]{:S(2)}) collective-permute-start(f32[256,2,128]{2,0,1:T(8,128)} %fusion.106), channel_id=1, source_target_pairs={{3,0},{0,1},{1,2},{2,3},{7,4},{4,5},{5,6},{6,7},{11,8},{8,9},{9,10... | collective-permute-start | bytes 786440 | tf_op jit(solution)/shard_map/while/body/eval_jaxpr/ppermute | solution.py:12
  110.5 12.0 %collective-permute-start = (bf16[256,2,128]{2,0,1:T(8,128)(2,1)S(1)}, bf16[256,2,128]{2,0,1:T(8,128)(2,1)}, u32[]{:S(2)}, u32[]{:S(2)}) collective-permute-start(bf16[256,2,128]{2,0,1:T(8,128)(2,1)S(1)} %copy.154), channel_id=1, source_target_pairs={{3,0},{0,1},{1,2},{2,3},{7,4},{4,5},{5,6},{6,7},{11,8},{8,9},{9,10... | collective-permute-start | bytes 393224 | tf_op jit(solution)/shard_map/while/body/eval_jaxpr/ppermute | solution.py:12
  111.4 11.1 %collective-permute-start.1 = (bf16[256,2,128]{2,0,1:T(8,128)(2,1)S(1)}, bf16[256,2,128]{2,0,1:T(8,128)(2,1)}, u32[]{:S(2)}, u32[]{:S(2)}) collective-permute-start(bf16[256,2,128]{2,0,1:T(8,128)(2,1)S(1)} %copy.155), channel_id=1, source_target_pairs={{3,0},{0,1},{1,2},{2,3},{7,4},{4,5},{5,6},{6,7},{11,8},{8,9},{9,10... | collective-permute-start | bytes 393224 | tf_op jit(solution)/shard_map/while/body/eval_jaxpr/ppermute | solution.py:12
  116.8 9.5 %collective-permute-start.2 = (f32[256,2,128]{2,0,1:T(8,128)}, f32[256,2,128]{2,0,1:T(8,128)}, u32[]{:S(2)}, u32[]{:S(2)}) collective-permute-start(f32[256,2,128]{2,0,1:T(8,128)} %fusion.105), channel_id=1, source_target_pairs={{3,0},{0,1},{1,2},{2,3},{7,4},{4,5},{5,6},{6,7},{11,8},{8,9},{9,10... | collective-permute-start | bytes 786440 | tf_op jit(solution)/shard_map/while/body/eval_jaxpr/ppermute | solution.py:12
  119.0 10.1 %collective-permute-start.3 = (f32[256,2,128]{2,0,1:T(8,128)}, f32[256,2,128]{2,0,1:T(8,128)}, u32[]{:S(2)}, u32[]{:S(2)}) collective-permute-start(f32[256,2,128]{2,0,1:T(8,128)} %fusion.106), channel_id=1, source_target_pairs={{3,0},{0,1},{1,2},{2,3},{7,4},{4,5},{5,6},{6,7},{11,8},{8,9},{9,10... | collective-permute-start | bytes 786440 | tf_op jit(solution)/shard_map/while/body/eval_jaxpr/ppermute | solution.py:12
  129.1 1.2 copy-start.2
  129.1 2.2 %copy-start.3 = (bf16[128,16,128]{2,1,0:T(8,128)(2,1)S(1)}, bf16[128,16,128]{2,1,0:T(8,128)(2,1)}, u32[]{:S(2)}) copy-start(bf16[128,16,128]{2,1,0:T(8,128)(2,1)} %param.19) | copy-start | bytes 1572868
  129.1 2.2 %copy-start.11 = (bf16[128]{0:T(256)(128)(2,1)S(1)}, bf16[128]{0:T(256)(128)(2,1)}, u32[]{:S(2)}) copy-start(bf16[128]{0:T(256)(128)(2,1)} %copy-done.10) | copy-start | bytes 772
where the time goes:
time: 137 us; the launch traced here: 136 us
  matrix products  36.8 us (27%)
  waiting for transfers between devices  26.5 us (19%)
  blocking collectives  23.6 us (17%)
  local copies, waits for them, and re-layouts  23.5 us (17%)
  starting transfers between devices  19.8 us (14%)
  other arithmetic  4.22 us (3%)
  between operations  1.61 us (1%)
    ppermute x16, waiting for transfers between devices, from_behind(): return lax.ppermute(block, axis, route)  26.5 us
    ppermute x16, starting transfers between devices, from_behind(): return lax.ppermute(block, axis, route)  19.8 us
    all_gather x1, blocking collectives, on_device(): block_values = lax.all_gather(prompt_v, 'blk', axis=0, tiled=True)  12.1 us
    all_gather x1, blocking collectives, on_device(): block_keys = lax.all_gather(prompt_k, 'blk', axis=0, tiled=True)  11.5 us
    dot_general x5, matrix products, back_terms(): jnp.einsum('kgrp,rkgd->pkd', weights_low, out_grad, preferred_element_typ...  9.09 us
    another operation x10, local copies, waits for them, and re-layouts  8.66 us
    dot_general x5, matrix products, back_terms(): jnp.einsum('kgrp,rkgd->pkd', dscore, grouped, preferred_element_type=jnp....  8.63 us
    dot_general x2, matrix products, value_per_block(): jnp.einsum('kgrp,pkd->rkgd', weights_low, values_now, preferred_element_t...  7.88 us
  transfers between devices with their start and end apart: 16, of which 8 were waited for; matrix products, arithmetic and copies ran while one was open for 21% of the time, Pallas kernels for 0%

commit v1 on v0

v1 whole, which is shorter than its diff:
```python
import functools
import math

import jax
import jax.numpy as jnp
from jax import lax
from jax.experimental import pallas as pl
from jax.experimental.pallas import tpu as pltpu
from jax.sharding import PartitionSpec as P

MESH = pl.DeviceIdType.MESH
BF16 = jnp.bfloat16
F32 = jnp.float32


def mm(a, b):
    return jnp.dot(a, b, preferred_element_type=F32)


def picks(shape, few, many, offset, group):
    one = lax.broadcasted_iota(jnp.int32, shape, few)
    other = lax.broadcasted_iota(jnp.int32, shape, many)
    return (other == group * one + offset).astype(F32).astype(BF16)


def split_heads(merged, group):
    if group == 1:
        return merged
    keys = merged.shape[0] // group
    shape = (keys, group * keys)
    parts = [mm(picks(shape, 0, 1, g, group), merged) for g in range(group)]
    return jnp.concatenate(parts, axis=1).astype(BF16)


def merge_heads(wide, group):
    if group == 1:
        return wide
    keys = wide.shape[0]
    dim = wide.shape[1] // group
    shape = (group * keys, keys)
    parts = [
        mm(picks(shape, 1, 0, g, group), wide[:, g * dim : (g + 1) * dim]) for g in range(group)
    ]
    return sum(parts[1:], parts[0]).astype(BF16)


def kernel(
    n, heads, group,
    live_ref, q_ref, k_ref, v_ref, rk_ref, rv_ref, do_ref, seg_ref,
    out_ref, dq_ref, drk_ref, drv_ref, dpk_ref, dpv_ref,
    kv, q_t, do_t, q_w, do_w, p_all, dp_all, p_loc, dp_loc, w_low, ds_low,
    mask_ref, o_acc, dq_acc, high, low_sum, factor_ref, delta_ref, loc_kv,
    g_out, g_in, send_sem, recv_sem, gsend_sem, grecv_sem,
):
    merged = q_ref.shape[0]
    dim = q_ref.shape[1]
    rows = merged // heads
    keys = k_ref.shape[0] // group
    rkeys = rk_ref.shape[0] // group
    width = 256
    chunks = merged // width
    scale = 1.0 / math.sqrt(dim)
    scale2 = scale * math.log2(math.e)
    me = lax.axis_index("blk")
    pair = n == 4
    if pair:
        xn = me + 1 - 2 * (me % 2)
        yn = (me + 2) % 4
        partners = [xn, yn]
    else:
        partners = [(me + s) % n for s in range(1, n)]

    barrier = pltpu.get_barrier_semaphore()
    for other in partners:
        pl.semaphore_signal(barrier, inc=1, device_id={"blk": other}, device_id_type=MESH)

    kv[0, 0] = split_heads(k_ref[...], group)
    kv[0, 1] = split_heads(v_ref[...], group)
    pl.semaphore_wait(barrier, len(partners))

    def move(src, dst, sem, other):
        return pltpu.make_async_remote_copy(
            src_ref=kv.at[src[0], src[1]], dst_ref=kv.at[dst[0], dst[1]],
            send_sem=send_sem.at[sem], recv_sem=recv_sem.at[sem],
            device_id={"blk": other}, device_id_type=MESH,
        )

    gather = {}
    if pair:
        gather["kx"] = move((0, 0), (1, 0), 0, xn)
        gather["vy"] = move((0, 1), (2, 1), 1, yn)
        gather["vx"] = move((0, 1), (1, 1), 2, xn)
        gather["ky"] = move((0, 0), (2, 0), 3, yn)
        gather["kd"] = move((1, 0), (3, 0), 4, yn)
        gather["vd"] = move((2, 1), (3, 1), 5, xn)
        for name in ("kx", "vy", "vx", "ky"):
            gather[name].start()
    else:
        for s in range(1, n):
            for t in range(2):
                gather[s, t] = move((0, t), (n - s, t), 2 * (n - s) + t, (me + s) % n)
                gather[s, t].start()

    live = live_ref[0]

    def lanes(c):
        return pl.ds(pl.multiple_of(c * width, width), width)

    def prepare(c, carry):
        at = lanes(c)
        row = lax.broadcasted_iota(jnp.int32, (width, dim), 0)
        owner = (row % heads) // (heads // group)
        alive = (row + c * width) // heads < live
        q = q_ref[at, :].astype(F32)
        do = jnp.where(alive, do_ref[at, :].astype(F32), 0.0)
        for value, wide, turned in ((q, q_w, q_t), (do, do_w, do_t)):
            for g in range(group):
                mine = jnp.where(owner == g, value, 0.0)
                span = slice(g * dim, (g + 1) * dim)
                wide[at, span] = mine.astype(BF16)
                turned[span, at] = mine.T.astype(BF16)
        return carry

    lax.fori_loop(0, chunks, prepare, 0)

    def own_head(wide):
        lane = lax.broadcasted_iota(jnp.int32, (dim, width), 1)
        owner = (lane % heads) // (heads // group)
        result = wide[:dim, :]
        for g in range(1, group):
            result = jnp.where(owner == g, wide[g * dim : (g + 1) * dim, :], result)
        return result

    def forward(index, key, value, p_store, dp_store, mask, first):
        value_t = value.astype(F32).T.astype(BF16)

        def step(c, carry):
            at = lanes(c)
            s = mm(key, q_t[:, at])
            if mask is not None:
                s = jnp.where(mask[:, at] > 0.5, s, -1e30)
            top = jnp.max(s, axis=0, keepdims=True)
            p = jnp.exp2((s - top) * scale2)
            p16 = p.astype(BF16)
            p_store[:, at] = p16
            dp_store[:, at] = mm(value, do_t[:, at]).astype(dp_store.dtype)
            o = own_head(mm(value_t, p16))
            total = jnp.sum(p, axis=0, keepdims=True)
            high[index + 1 : index + 2, at] = top
            if first:
                high[0:1, at] = top
                low_sum[0:1, at] = total
                o_acc[:, at] = o
            else:
                old = high[0:1, at]
                new = jnp.maximum(old, top)
                keep = jnp.exp2((old - new) * scale2)
                gain = jnp.exp2((top - new) * scale2)
                high[0:1, at] = new
                low_sum[0:1, at] = low_sum[0:1, at] * keep + total * gain
                o_acc[:, at] = o_acc[:, at] * keep + o * gain
            return carry

        lax.fori_loop(0, chunks, step, 0)

    def forward_slot(s, first=False):
        forward(s, kv[s, 0], kv[s, 1], p_all.at[s], dp_all.at[s], None, first)

    forward_slot(0, True)
    if pair:
        gather["kx"].wait_recv()
        gather["kd"].start()
        gather["vy"].wait_recv()
        gather["vd"].start()

    seg = seg_ref[...].astype(F32)
    ri = lax.broadcasted_iota(jnp.int32, (rkeys, rkeys), 0)
    ci = lax.broadcasted_iota(jnp.int32, (rkeys, rkeys), 1)
    seg_row = jnp.broadcast_to(seg, (rkeys, rkeys))
    seg_col = jnp.sum(jnp.where(ri == ci, seg_row, 0.0), axis=1, keepdims=True)
    allowed = jnp.where((ri <= ci) & (seg_col == seg_row), 1.0, 0.0).astype(BF16)
    er = lax.broadcasted_iota(jnp.int32, (rkeys, merged), 0)
    ec = lax.broadcasted_iota(jnp.int32, (rkeys, merged), 1)
    expand = (er == ec // heads).astype(F32).astype(BF16)
    mask_ref[...] = mm(allowed, expand)
    loc_kv[0] = split_heads(rk_ref[...], group)
    loc_kv[1] = split_heads(rv_ref[...], group)
    forward(n, loc_kv[0], loc_kv[1], p_loc, dp_loc, mask_ref, False)

    if pair:
        gather["vx"].wait_recv()
        forward_slot(1)
        gather["ky"].wait_recv()
        forward_slot(2)
        gather["kd"].wait_recv()
        gather["vd"].wait_recv()
        forward_slot(3)
    else:
        for s in range(n - 1, 0, -1):
            gather[s, 0].wait_recv()
            gather[s, 1].wait_recv()
            forward_slot(n - s)

    def finish(c, carry):
        at = lanes(c)
        inverse = 1.0 / low_sum[0:1, at]
        lane = lax.broadcasted_iota(jnp.int32, (1, width), 1) + c * width
        alive = (lane // heads) < live
        o16 = jnp.where(alive, o_acc[:, at] * inverse, 0.0).astype(BF16)
        o = o16.astype(F32)
        out_ref[at, :] = o.T.astype(BF16)
        do = own_head(do_t[:, at].astype(F32))
        delta_ref[0:1, at] = jnp.sum(do * o, axis=0, keepdims=True)
        top = high[0:1, at]
        for s in range(n + 1):
            factor_ref[s : s + 1, at] = (
                jnp.exp2((high[s + 1 : s + 2, at] - top) * scale2) * inverse
            )
        return carry

    lax.fori_loop(0, chunks, finish, 0)

    def backward(index, key, p_store, dp_store, first):
        key_t = key.astype(F32).T.astype(BF16)
        count = key.shape[0]

        def step(c, carry):
            at = lanes(c)
            w = p_store[:, at].astype(F32) * factor_ref[index : index + 1, at]
            w_low[:count, at] = w.astype(BF16)
            ds = (w * (dp_store[:, at].astype(F32) - delta_ref[0:1, at]) * scale).astype(BF16)
            ds_low[:count, at] = ds
            part = own_head(mm(key_t, ds))
            if first:
                dq_acc[:, at] = part
            else:
                dq_acc[:, at] += part
            return carry

        lax.fori_loop(0, chunks, step, 0)
        return mm(ds_low[:count, :], q_w[...]), mm(w_low[:count, :], do_w[...])

    def backward_slot(s, first=False):
        return backward(s, kv[s, 0], p_all.at[s], dp_all.at[s], first)

    def give(slot, other):
        return pltpu.make_async_remote_copy(
            src_ref=g_out.at[slot], dst_ref=g_in.at[slot],
            send_sem=gsend_sem.at[slot], recv_sem=grecv_sem.at[slot],
            device_id={"blk": other}, device_id_type=MESH,
        )

    back = []
    if pair:
        gk, gv = backward_slot(3, True)
        g_out[0] = gk.astype(BF16)
        kd = give(0, xn)
        kd.start()
        g_out[1] = gv.astype(BF16)
        vd = give(1, yn)
        vd.start()
        gk, gv = backward_slot(1)
        g_out[2] = gk.astype(BF16)
        kx = give(2, xn)
        kx.start()
        vd.wait_recv()
        g_out[3] = (gv + g_in[1].astype(F32)).astype(BF16)
        vx = give(3, xn)
        vx.start()
        gk, gv = backward_slot(2)
        g_out[4] = gv.astype(BF16)
        vy = give(4, yn)
        vy.start()
        kd.wait_recv()
        g_out[5] = (gk + g_in[0].astype(F32)).astype(BF16)
        ky = give(5, yn)
        ky.start()
        back = [kd, vd, kx, vx, vy, ky]
    else:
        for s in range(1, n):
            gk, gv = backward_slot(s, s == 1)
            g_out[2 * s] = gk.astype(BF16)
            g_out[2 * s + 1] = gv.astype(BF16)
            for t in range(2):
                back.append(give(2 * s + t, (me + s) % n))
                back[-1].start()

    gk, gv = backward(n, loc_kv[0], p_loc, dp_loc, False)
    drk_ref[...] = merge_heads(gk.astype(BF16), group)
    drv_ref[...] = merge_heads(gv.astype(BF16), group)
    gk, gv = backward_slot(0)

    def last(c, carry):
        at = lanes(c)
        dq_ref[at, :] = dq_acc[:, at].T.astype(BF16)
        return carry

    lax.fori_loop(0, chunks, last, 0)

    if pair:
        kx.wait_recv()
        vy.wait_recv()
        vx.wait_recv()
        ky.wait_recv()
        gk = gk + g_in[2].astype(F32) + g_in[5].astype(F32)
        gv = gv + g_in[4].astype(F32) + g_in[3].astype(F32)
    else:
        for s in range(1, n):
            back[2 * s - 2].wait_recv()
            back[2 * s - 1].wait_recv()
            gk = gk + g_in[2 * s].astype(F32)
            gv = gv + g_in[2 * s + 1].astype(F32)
    dpk_ref[...] = merge_heads(gk.astype(BF16), group)
    dpv_ref[...] = merge_heads(gv.astype(BF16), group)
    for copy in list(gather.values()) + back:
        copy.wait_send()


def on_device(n, resp_q, prompt_k, prompt_v, resp_k, resp_v, d_out, segment_ids, live_rows):
    rows, heads, dim = resp_q.shape
    keys, kvh, _ = prompt_k.shape
    rkeys = resp_k.shape[0]
    merged = rows * heads
    flat = lambda a: a.reshape(-1, dim)
    vmem = pl.BlockSpec(memory_space=pltpu.VMEM)
    dp_type = F32 if n <= 4 else BF16
    stats = ((n + 2 + 7) // 8) * 8
    grads = 6 if n == 4 else 2 * n
    results = pl.pallas_call(
        functools.partial(kernel, n, heads, kvh),
        out_shape=[
            jax.ShapeDtypeStruct((merged, dim), BF16),
            jax.ShapeDtypeStruct((merged, dim), BF16),
            jax.ShapeDtypeStruct((rkeys * kvh, dim), BF16),
            jax.ShapeDtypeStruct((rkeys * kvh, dim), BF16),
            jax.ShapeDtypeStruct((keys * kvh, dim), BF16),
            jax.ShapeDtypeStruct((keys * kvh, dim), BF16),
        ],
        in_specs=[pl.BlockSpec(memory_space=pltpu.SMEM)] + [vmem] * 7,
        out_specs=[vmem] * 6,
        scratch_shapes=[
            pltpu.VMEM((n, 2, keys, kvh * dim), BF16),
            pltpu.VMEM((kvh * dim, merged), BF16),
            pltpu.VMEM((kvh * dim, merged), BF16),
            pltpu.VMEM((merged, kvh * dim), BF16),
            pltpu.VMEM((merged, kvh * dim), BF16),
            pltpu.VMEM((n, keys, merged), BF16),
            pltpu.VMEM((n, keys, merged), dp_type),
            pltpu.VMEM((rkeys, merged), BF16),
            pltpu.VMEM((rkeys, merged), dp_type),
            pltpu.VMEM((keys, merged), BF16),
            pltpu.VMEM((keys, merged), BF16),
            pltpu.VMEM((rkeys, merged), F32),
            pltpu.VMEM((dim, merged), F32),
            pltpu.VMEM((dim, merged), F32),
            pltpu.VMEM((stats, merged), F32),
            pltpu.VMEM((8, merged), F32),
            pltpu.VMEM((stats, merged), F32),
            pltpu.VMEM((8, merged), F32),
            pltpu.VMEM((2, rkeys, kvh * dim), BF16),
            pltpu.VMEM((grads, keys, kvh * dim), BF16),
            pltpu.VMEM((grads, keys, kvh * dim), BF16),
            pltpu.SemaphoreType.DMA((2 * n,)),
            pltpu.SemaphoreType.DMA((2 * n,)),
            pltpu.SemaphoreType.DMA((grads,)),
            pltpu.SemaphoreType.DMA((grads,)),
        ],
        compiler_params=pltpu.CompilerParams(
            collective_id=0, has_side_effects=True, vmem_limit_bytes=60 * 1024 * 1024
        ),
        cost_estimate=pl.CostEstimate(
            flops=12 * merged * dim * (n * keys + rkeys),
            bytes_accessed=4 * merged * dim * 2,
            transcendentals=merged * (n * keys + rkeys),
        ),
    )(
        live_rows, flat(resp_q), flat(prompt_k), flat(prompt_v), flat(resp_k), flat(resp_v),
        flat(d_out), segment_ids,
    )
    shapes = (resp_q, resp_q, resp_k, resp_v, prompt_k, prompt_v)
    return tuple(r.reshape(s.shape) for r, s in zip(results, shapes))


def solution(mesh):
    split = P(("group", "blk"), "kvh", None)
    return jax.shard_map(
        functools.partial(on_device, mesh.shape["blk"]),
        mesh=mesh,
        in_specs=(split,) * 6 + (P(("group", "blk"), None), P(("group", "blk"))),
        out_specs=(split,) * 6,
        check_vma=False,
    )
```

time: 137 us -> 52.4 us (0.38)
  Pallas kernels: 0 us -> 45.2 us
  matrix products: 36.8 us -> 0 us
  waiting for transfers between devices: 26.5 us -> 0 us
  blocking collectives: 23.6 us -> 0 us
  starting transfers between devices: 19.8 us -> 0 us
  local copies, waits for them, and re-layouts: 23.5 us -> 5.66 us
  other arithmetic: 4.22 us -> 0 us
    pallas_call x0 -> x1, Pallas kernels: none -> 45.2 us  [on_device(): pl.pallas_call(functools.partial(kernel, n, heads, kvh), out_shape=[jax.S...]
    dot_general x30 -> x0, matrix products: 36.8 us -> none  [the longest x5 9.09 us: back_terms(): jnp.einsum('kgrp,rkgd->pkd', weights_low, out_grad, preferred_element_typ...]
    ppermute x16 -> x0, waiting for transfers between devices: 26.5 us -> none  [from_behind(): return lax.ppermute(block, axis, route)]
    all_gather x2 -> x0, blocking collectives: 23.6 us -> none  [the longest x1 12.1 us: on_device(): block_values = lax.all_gather(prompt_v, 'blk', axis=0, tiled=True)]
    ppermute x16 -> x0, starting transfers between devices: 19.8 us -> none  [from_behind(): return lax.ppermute(block, axis, route)]
    while x8 -> x0, local copies, waits for them, and re-layouts: 9.05 us -> none  [the longest x4 4.94 us: on_device(): lax.fori_loop(0, devices, one_turn, (prompt_k, prompt_v, zero_grad, zero_...]
    another operation x10 -> x0, local copies, waits for them, and re-layouts: 8.66 us -> none
    unnamed x32 -> x16, local copies, waits for them, and re-layouts: 2.69 us -> 5.66 us
  transfers between devices with their start and end apart: 16 -> 0, of which waited for: 8 -> 0; matrix products, arithmetic and copies ran while one was open for 21% -> 0% of each run, Pallas kernels for 0% -> 0%
where the time goes in v1:
time: 52.4 us; the launch traced here: 52.1 us
  Pallas kernels  45.2 us (86%)
  local copies, waits for them, and re-layouts  5.66 us (11%)
  between operations  1.3 us (2%)
    pallas_call x1, Pallas kernels, on_device(): pl.pallas_call(functools.partial(kernel, n, heads, kvh), out_shape=[jax.S...  45.2 us
    unnamed x16, local copies, waits for them, and re-layouts  5.66 us

profile of v1, /device:TPU:0, one launch (start us, length us, event | category | flops | bytes accessed | tf_op | source)
XLA Modules:
  0.0 52.1 jit_solution(3818144312376809915)
XLA Ops:
  1.3 45.2 %shard_map.127 = (bf16[2048,128]{1,0:T(8,128)(2,1)}, bf16[2048,128]{1,0:T(8,128)(2,1)}, bf16[256,128]{1,0:T(8,128)(2,1)}, bf16[256,128]{1,0:T(8,128)(2,1)}, bf16...) custom-call(s32[1]{0:T(128)S(6)} %copy.20.live_ref, bf16[2048,128]{1,0:T(8,128)(2,1)} %bitcast.18, ...), custom_call_target="tpu_custom_call" | custom-call | flops 3623878656 | bytes 2097152 | tf_op jit(solution)/shard_map/pallas_call | solution.py:329
  46.5 0.0 copy-start
  46.5 1.9 %copy.21 = bf16[128,16,128]{2,1,0:T(8,128)(2,1)} copy(bf16[128,16,128]{2,1,0:T(8,128)(2,1)} %bitcast.13) | data formatting | bytes 1048576
  48.4 0.0 copy-done
  48.4 0.0 copy-start.4
  48.4 0.0 copy-start.3
  48.4 0.8 %copy.22 = bf16[128,16,128]{2,1,0:T(8,128)(2,1)} copy(bf16[128,16,128]{2,1,0:T(8,128)(2,1)S(1)} %bitcast.12) | data formatting | bytes 1048576
  49.2 0.1 copy-done.4
  49.3 0.0 copy-start.2
  49.3 0.6 %copy.23 = bf16[128,2,128]{2,1,0:T(2,128)(2,1)} copy(bf16[128,2,128]{2,1,0:T(2,128)(2,1)S(1)} %bitcast.17) | data formatting | bytes 131072
  49.9 0.0 copy-done.3
  49.9 0.6 %copy.24 = bf16[128,2,128]{2,1,0:T(2,128)(2,1)} copy(bf16[128,2,128]{2,1,0:T(2,128)(2,1)S(1)} %bitcast.16) | data formatting | bytes 131072
  50.5 0.0 copy-done.2
  50.5 0.0 copy-start.1
  50.5 0.7 %copy.25 = bf16[256,2,128]{2,1,0:T(2,128)(2,1)} copy(bf16[256,2,128]{2,1,0:T(2,128)(2,1)S(1)} %bitcast.15) | data formatting | bytes 262144
  51.2 0.3 copy-done.1
  51.5 0.7 %copy.26 = bf16[256,2,128]{2,1,0:T(2,128)(2,1)} copy(bf16[256,2,128]{2,1,0:T(2,128)(2,1)S(1)} %bitcast.14) | data formatting | bytes 262144
Async XLA Ops:
  46.5 1.9 %copy-start = (bf16[2048,128]{1,0:T(8,128)(2,1)S(1)}, bf16[2048,128]{1,0:T(8,128)(2,1)}, u32[]{:S(2)}) copy-start(bf16[2048,128]{1,0:T(8,128)(2,1)} %get-tuple-element.13) | copy-start | bytes 1572868
  48.4 0.9 %copy-start.4 = (bf16[256,128]{1,0:T(8,128)(2,1)S(1)}, bf16[256,128]{1,0:T(8,128)(2,1)}, u32[]{:S(2)}) copy-start(bf16[256,128]{1,0:T(8,128)(2,1)} %get-tuple-element.14) | copy-start | bytes 196612
  48.4 1.5 %copy-start.3 = (bf16[256,128]{1,0:T(8,128)(2,1)S(1)}, bf16[256,128]{1,0:T(8,128)(2,1)}, u32[]{:S(2)}) copy-start(bf16[256,128]{1,0:T(8,128)(2,1)} %get-tuple-element.15) | copy-start | bytes 196612
  49.3 1.3 %copy-start.2 = (bf16[512,128]{1,0:T(8,128)(2,1)S(1)}, bf16[512,128]{1,0:T(8,128)(2,1)}, u32[]{:S(2)}) copy-start(bf16[512,128]{1,0:T(8,128)(2,1)} %get-tuple-element.16) | copy-start | bytes 393220
  50.5 1.0 %copy-start.1 = (bf16[512,128]{1,0:T(8,128)(2,1)S(1)}, bf16[512,128]{1,0:T(8,128)(2,1)}, u32[]{:S(2)}) copy-start(bf16[512,128]{1,0:T(8,128)(2,1)} %get-tuple-element.17) | copy-start | bytes 393220

commit v2 on v1

--- a/solution.py
+++ b/solution.py
@@ -11,6 +11,9 @@
 MESH = pl.DeviceIdType.MESH
 BF16 = jnp.bfloat16
 F32 = jnp.float32
+FWD_UNROLL = 8
+BWD_UNROLL = 8
+PREP_UNROLL = 2
 
 
 def mm(a, b):
@@ -121,7 +124,7 @@
                 turned[span, at] = mine.T.astype(BF16)
         return carry
 
-    lax.fori_loop(0, chunks, prepare, 0)
+    lax.fori_loop(0, chunks, prepare, 0, unroll=PREP_UNROLL)
 
     def own_head(wide):
         lane = lax.broadcasted_iota(jnp.int32, (dim, width), 1)
@@ -161,7 +164,7 @@
                 o_acc[:, at] = o_acc[:, at] * keep + o * gain
             return carry
 
-        lax.fori_loop(0, chunks, step, 0)
+        lax.fori_loop(0, chunks, step, 0, unroll=FWD_UNROLL)
 
     def forward_slot(s, first=False):
         forward(s, kv[s, 0], kv[s, 1], p_all.at[s], dp_all.at[s], None, first)
@@ -218,7 +221,7 @@
             )
         return carry
 
-    lax.fori_loop(0, chunks, finish, 0)
+    lax.fori_loop(0, chunks, finish, 0, unroll=PREP_UNROLL)
 
     def backward(index, key, p_store, dp_store, first):
         key_t = key.astype(F32).T.astype(BF16)
@@ -237,7 +240,7 @@
                 dq_acc[:, at] += part
             return carry
 
-        lax.fori_loop(0, chunks, step, 0)
+        lax.fori_loop(0, chunks, step, 0, unroll=BWD_UNROLL)
         return mm(ds_low[:count, :], q_w[...]), mm(w_low[:count, :], do_w[...])
 
     def backward_slot(s, first=False):
@@ -295,7 +298,7 @@
         dq_ref[at, :] = dq_acc[:, at].T.astype(BF16)
         return carry
 
-    lax.fori_loop(0, chunks, last, 0)
+    lax.fori_loop(0, chunks, last, 0, unroll=PREP_UNROLL)
 
     if pair:
         kx.wait_recv()
@@ -314,6 +317,22 @@
     dpv_ref[...] = merge_heads(gv.astype(BF16), group)
     for copy in list(gather.values()) + back:
         copy.wait_send()
+
+
+def store_kernel(*refs):
+    count = len(refs) // 2
+    for i in range(count):
+        refs[count + i][...] = refs[i][...]
+
+
+def store(results):
+    vmem = pl.BlockSpec(memory_space=pltpu.VMEM)
+    return pl.pallas_call(
+        store_kernel,
+        out_shape=[jax.ShapeDtypeStruct(r.shape, r.dtype) for r in results],
+        in_specs=[vmem] * len(results),
+        out_specs=[vmem] * len(results),
+    )(*results)
 
 
 def on_device(n, resp_q, prompt_k, prompt_v, resp_k, resp_v, d_out, segment_ids, live_rows):
@@ -377,6 +396,7 @@
         live_rows, flat(resp_q), flat(prompt_k), flat(prompt_v), flat(resp_k), flat(resp_v),
         flat(d_out), segment_ids,
     )
+    results = store(results)
     shapes = (resp_q, resp_q, resp_k, resp_v, prompt_k, prompt_v)
     return tuple(r.reshape(s.shape) for r, s in zip(results, shapes))
 

time: 52.4 us -> 38.4 us (0.73)
  Pallas kernels: 45.2 us -> 36.9 us
  local copies, waits for them, and re-layouts: 5.66 us -> 0 us
    pallas_call x1, Pallas kernels: 45.2 us -> 34.5 us  [on_device(): pl.pallas_call(functools.partial(kernel, n, heads, kvh), out_shape=[jax.S...]
    unnamed x16 -> x0, local copies, waits for them, and re-layouts: 5.66 us -> none
    pallas_call x0 -> x1, Pallas kernels: none -> 2.42 us  [store(): pl.pallas_call(store_kernel, out_shape=[jax.ShapeDtypeStruct(r.shape, r.d...]
where the time goes in v2:
time: 38.4 us; the launch traced here: 38.2 us
  Pallas kernels  36.9 us (96%)
  between operations  1.29 us (3%)
    pallas_call x1, Pallas kernels, on_device(): pl.pallas_call(functools.partial(kernel, n, heads, kvh), out_shape=[jax.S...  34.5 us
    pallas_call x1, Pallas kernels, store(): pl.pallas_call(store_kernel, out_shape=[jax.ShapeDtypeStruct(r.shape, r.d...  2.42 us

profile of v2, /device:TPU:0, one launch (start us, length us, event | category | flops | bytes accessed | tf_op | source)
XLA Modules:
  0.0 38.2 jit_solution(17581988239257611825)
XLA Ops:
  1.3 34.5 %shard_map.127 = (bf16[2048,128]{1,0:T(8,128)(2,1)}, bf16[2048,128]{1,0:T(8,128)(2,1)}, bf16[256,128]{1,0:T(8,128)(2,1)}, bf16[256,128]{1,0:T(8,128)(2,1)}, bf16...) custom-call(s32[1]{0:T(128)S(6)} %copy.14.live_ref, bf16[2048,128]{1,0:T(8,128)(2,1)} %bitcast.12, ...), custom_call_target="tpu_custom_call" | custom-call | flops 3623878656 | bytes 2097152 | tf_op jit(solution)/shard_map/pallas_call | solution.py:348
  35.8 2.4 %shard_map.128 = (bf16[2048,128]{1,0:T(8,128)(2,1)}, bf16[2048,128]{1,0:T(8,128)(2,1)}, bf16[256,128]{1,0:T(8,128)(2,1)}, bf16[256,128]{1,0:T(8,128)(2,1)}, bf16...) custom-call(bf16[2048,128]{1,0:T(8,128)(2,1)} %get-tuple-element.18.refs_0_, bf16[2048,128]{1,0:T(8,128)(2,1)} %get-tuple-element.19.refs_1_, ...), custom_call_target="tpu_custom_call" | custom-call | tf_op jit(solution)/shard_map/pallas_call | solution.py:330

commit v3 on v2

v3 whole, which is shorter than its diff:
```python
import functools
import math

import jax
import jax.numpy as jnp
from jax import lax
from jax.experimental import pallas as pl
from jax.experimental.pallas import tpu as pltpu
from jax.sharding import PartitionSpec as P

MESH = pl.DeviceIdType.MESH
BF16 = jnp.bfloat16
F32 = jnp.float32
UNROLL = 8
PREP_UNROLL = 2


def mm(a, b):
    return jnp.dot(a, b, preferred_element_type=F32)


def picks(shape, few, many, offset, group):
    one = lax.broadcasted_iota(jnp.int32, shape, few)
    other = lax.broadcasted_iota(jnp.int32, shape, many)
    return (other == group * one + offset).astype(F32).astype(BF16)


def split_heads(merged, group):
    if group == 1:
        return merged
    keys = merged.shape[0] // group
    shape = (keys, group * keys)
    parts = [mm(picks(shape, 0, 1, g, group), merged) for g in range(group)]
    return jnp.concatenate(parts, axis=1).astype(BF16)


def merge_heads(wide, group):
    if group == 1:
        return wide
    keys = wide.shape[0]
    dim = wide.shape[1] // group
    shape = (group * keys, keys)
    parts = [
        mm(picks(shape, 1, 0, g, group), wide[:, g * dim : (g + 1) * dim]) for g in range(group)
    ]
    return sum(parts[1:], parts[0]).astype(BF16)


def kernel(
    n, heads, group,
    live_ref, q_ref, k_ref, v_ref, rk_ref, rv_ref, do_ref, seg_ref,
    out_ref, dq_ref, drk_ref, drv_ref, dpk_ref, dpv_ref,
    kv, q_t, do_t, q_w, do_w, w_all, w_loc, ds_low, mask_ref, o_acc, dq_acc,
    high, totals, delta_ref, loc_kv, v_turned, own_grad, hold,
    g_out, g_in, send_sem, recv_sem, gsend_sem, grecv_sem,
):
    merged = q_ref.shape[0]
    dim = q_ref.shape[1]
    keys = k_ref.shape[0] // group
    rkeys = rk_ref.shape[0] // group
    half = keys // 2
    width = 256
    chunks = merged // width
    scale = 1.0 / math.sqrt(dim)
    scale2 = scale * math.log2(math.e)
    me = lax.axis_index("blk")
    pair = n == 4
    if pair:
        xn = me + 1 - 2 * (me % 2)
        yn = (me + 2) % 4
        partners = [xn, yn]
    else:
        partners = [(me + s) % n for s in range(1, n)]

    barrier = pltpu.get_barrier_semaphore()
    for other in partners:
        pl.semaphore_signal(barrier, inc=1, device_id={"blk": other}, device_id_type=MESH)
    kv[0, 0] = split_heads(k_ref[...], group)
    kv[0, 1] = split_heads(v_ref[...], group)
    pl.semaphore_wait(barrier, len(partners))

    def move(src, dst, t, span, sem, other):
        return pltpu.make_async_remote_copy(
            src_ref=kv.at[src, t, span], dst_ref=kv.at[dst, t, span],
            send_sem=send_sem.at[sem], recv_sem=recv_sem.at[sem],
            device_id={"blk": other}, device_id_type=MESH,
        )

    low, upper, full = pl.ds(0, half), pl.ds(half, half), pl.ds(0, keys)
    gather = {}
    for t in range(2):
        if pair:
            gather[t, "lx"] = move(0, 1, t, low, 6 * t, xn)
            gather[t, "uy"] = move(0, 2, t, upper, 6 * t + 1, yn)
            gather[t, "ux"] = move(0, 1, t, upper, 6 * t + 2, xn)
            gather[t, "ly"] = move(0, 2, t, low, 6 * t + 3, yn)
            gather[t, "ld"] = move(1, 3, t, low, 6 * t + 4, yn)
            gather[t, "ud"] = move(2, 3, t, upper, 6 * t + 5, xn)
        else:
            for s in range(1, n):
                gather[t, s] = move(0, n - s, t, full, 2 * (n - s) + t, (me + s) % n)

    def begin(t):
        for name in ("lx", "uy", "ux", "ly") if pair else range(1, n):
            gather[t, name].start()

    def forward(t):
        if pair:
            gather[t, "lx"].wait_recv()
            gather[t, "ld"].start()
            gather[t, "uy"].wait_recv()
            gather[t, "ud"].start()

    def arrived(t, slot):
        if pair:
            for name in {1: ("ux",), 2: ("ly",), 3: ("ld", "ud")}[slot]:
                gather[t, name].wait_recv()
        else:
            gather[t, n - slot].wait_recv()

    begin(0)
    live = live_ref[0]

    def lanes(c):
        return pl.ds(pl.multiple_of(c * width, width), width)

    def loop(step, unroll):
        lax.fori_loop(0, chunks, lambda c, carry: step(c, lanes(c)), None, unroll=unroll)

    def prepare(c, at):
        row = lax.broadcasted_iota(jnp.int32, (width, dim), 0)
        owner = (row % heads) // (heads // group)
        alive = (row + c * width) // heads < live
        q = q_ref[at, :].astype(F32)
        do = jnp.where(alive, do_ref[at, :].astype(F32), 0.0)
        for value, wide, turned in ((q, q_w, q_t), (do, do_w, do_t)):
            for g in range(group):
                mine = jnp.where(owner == g, value, 0.0)
                span = slice(g * dim, (g + 1) * dim)
                wide[at, span] = mine.astype(BF16)
                turned[span, at] = mine.T.astype(BF16)

    loop(prepare, PREP_UNROLL)

    def own_head(wide):
        lane = lax.broadcasted_iota(jnp.int32, (dim, width), 1)
        owner = (lane % heads) // (heads // group)
        result = wide[:dim, :]
        for g in range(1, group):
            result = jnp.where(owner == g, wide[g * dim : (g + 1) * dim, :], result)
        return result

    def keys_of(s):
        return loc_kv[0] if s == n else kv[s, 0]

    def values_of(s):
        return loc_kv[1] if s == n else kv[s, 1]

    def weights_of(s):
        return w_loc if s == n else w_all.at[s]

    def exponentials(s):
        key = keys_of(s)
        store = weights_of(s)

        def step(c, at):
            score = mm(key, q_t[:, at])
            if s == n:
                score = jnp.where(mask_ref[:, at] > 0.5, score, -1e30)
            top = jnp.max(score, axis=0, keepdims=True)
            p = jnp.exp2((score - top) * scale2)
            store[:, at] = p.astype(BF16)
            high[s : s + 1, at] = top
            totals[s : s + 1, at] = jnp.sum(p, axis=0, keepdims=True)

        loop(step, UNROLL)

    exponentials(0)
    forward(0)
    begin(1)

    seg = seg_ref[...].astype(F32)
    ri = lax.broadcasted_iota(jnp.int32, (rkeys, rkeys), 0)
    ci = lax.broadcasted_iota(jnp.int32, (rkeys, rkeys), 1)
    seg_row = jnp.broadcast_to(seg, (rkeys, rkeys))
    seg_col = jnp.sum(jnp.where(ri == ci, seg_row, 0.0), axis=1, keepdims=True)
    allowed = jnp.where((ri <= ci) & (seg_col == seg_row), 1.0, 0.0).astype(BF16)
    er = lax.broadcasted_iota(jnp.int32, (rkeys, merged), 0)
    ec = lax.broadcasted_iota(jnp.int32, (rkeys, merged), 1)
    expand = (er == ec // heads).astype(F32).astype(BF16)
    mask_ref[...] = mm(allowed, expand)
    loc_kv[0] = split_heads(rk_ref[...], group)
    loc_kv[1] = split_heads(rv_ref[...], group)
    exponentials(n)
    for s in range(1, n):
        arrived(0, s)
        exponentials(s)

    def factors(c, at):
        tops = high[0 : n + 1, at]
        gain = jnp.exp2((tops - jnp.max(tops, axis=0, keepdims=True)) * scale2)
        total = jnp.sum(gain * totals[0 : n + 1, at], axis=0, keepdims=True)
        totals[0 : n + 1, at] = gain * (1.0 / total)

    loop(factors, PREP_UNROLL)

    def value_grad(s):
        store = weights_of(s)

        def step(c, at):
            w = store[:, at].astype(F32) * totals[s : s + 1, at]
            store[:, at] = w.astype(BF16)

        loop(step, UNROLL)
        return mm(store[...], do_w[...])

    def key_grad(s, first):
        key_t = keys_of(s).astype(F32).T.astype(BF16)
        value = values_of(s)
        store = weights_of(s)
        count = key_t.shape[1]

        def step(c, at):
            dprob = mm(value, do_t[:, at])
            ds = (store[:, at].astype(F32) * (dprob - delta_ref[0:1, at])).astype(BF16)
            ds_low[:count, at] = ds
            part = own_head(mm(key_t, ds))
            if first:
                dq_acc[:, at] = part
            else:
                dq_acc[:, at] += part

        loop(step, UNROLL)
        return mm(ds_low[:count, :], q_w[...]) * scale

    count = 6 if pair else n

    def give(t, slot, other):
        at = t * count + slot
        return pltpu.make_async_remote_copy(
            src_ref=g_out.at[at], dst_ref=g_in.at[at],
            send_sem=gsend_sem.at[at], recv_sem=grecv_sem.at[at],
            device_id={"blk": other}, device_id_type=MESH,
        )

    back = {}

    def send(t, slot, other, value):
        g_out[t * count + slot] = value.astype(BF16)
        back[t, slot] = give(t, slot, other)
        back[t, slot].start()

    def received(t, slot):
        back[t, slot].wait_recv()
        return g_in[t * count + slot].astype(F32)

    def direct(t, s, grad):
        if not pair:
            send(t, s, (me + s) % n, grad)
        elif s == 3:
            send(t, 0, xn, grad[:half])
            send(t, 1, yn, grad[half:])
        elif s == 1:
            send(t, 2, xn, grad[:half])
            hold[0] = grad[half:]
        else:
            send(t, 4, yn, grad[half:])
            hold[1] = grad[:half]

    def combined(t):
        if pair:
            send(t, 3, xn, hold[0] + received(t, 1))
            send(t, 5, yn, hold[1] + received(t, 0))

    def total_of(t, own):
        if pair:
            lower = own[:half] + received(t, 2) + received(t, 5)
            higher = own[half:] + received(t, 4) + received(t, 3)
            return jnp.concatenate([lower, higher], axis=0)
        for s in range(1, n):
            own = own + received(t, s)
        return own

    order = [3, 1, 2] if pair else list(range(1, n))
    for s in order:
        direct_grad = value_grad(s)
        if s == order[0]:
            forward(1)
        direct(0, s, direct_grad)
    drv_ref[...] = merge_heads(value_grad(n).astype(BF16), group)
    own_grad[...] = value_grad(0)

    def turn_values(s):
        value_t = values_of(s).astype(F32).T.astype(BF16)
        if s == n:
            v_turned[n, :, :rkeys] = value_t
        else:
            v_turned[s] = value_t

    def output_part(slots, at):
        total = None
        for s in slots:
            turned = v_turned[n, :, :rkeys] if s == n else v_turned[s]
            part = mm(turned, weights_of(s)[:, at])
            total = part if total is None else total + part
        return own_head(total)

    early = [0, n, 1, 2] if pair else [0, n]
    late = [3] if pair else list(range(1, n))
    for s in early:
        if 0 < s < n:
            arrived(1, s)
        turn_values(s)

    def begin_output(c, at):
        o_acc[:, at] = output_part(early, at)

    loop(begin_output, PREP_UNROLL)
    for s in late:
        arrived(1, s)
        turn_values(s)

    def finish(c, at):
        lane = lax.broadcasted_iota(jnp.int32, (1, width), 1) + c * width
        alive = (lane // heads) < live
        o = o_acc[:, at] + output_part(late, at)
        o = jnp.where(alive, o, 0.0).astype(BF16).astype(F32)
        out_ref[at, :] = o.T.astype(BF16)
        do = own_head(do_t[:, at].astype(F32))
        delta_ref[0:1, at] = jnp.sum(do * o, axis=0, keepdims=True)

    loop(finish, PREP_UNROLL)
    combined(0)
    for s in order:
        direct(1, s, key_grad(s, s == order[0]))
    drk_ref[...] = merge_heads(key_grad(n, False).astype(BF16), group)
    combined(1)
    own_key = key_grad(0, False)

    def last(c, at):
        dq_ref[at, :] = (dq_acc[:, at] * scale).T.astype(BF16)

    loop(last, PREP_UNROLL)
    dpv_ref[...] = merge_heads(total_of(0, own_grad[...]).astype(BF16), group)
    dpk_ref[...] = merge_heads(total_of(1, own_key).astype(BF16), group)
    for copy in list(gather.values()) + list(back.values()):
        copy.wait_send()


def store_kernel(*refs):
    count = len(refs) // 2
    for i in range(count):
        refs[count + i][...] = refs[i][...]


def store(results):
    vmem = pl.BlockSpec(memory_space=pltpu.VMEM)
    return pl.pallas_call(
        store_kernel,
        out_shape=[jax.ShapeDtypeStruct(r.shape, r.dtype) for r in results],
        in_specs=[vmem] * len(results),
        out_specs=[vmem] * len(results),
    )(*results)


def on_device(n, resp_q, prompt_k, prompt_v, resp_k, resp_v, d_out, segment_ids, live_rows):
    rows, heads, dim = resp_q.shape
    keys, kvh, _ = prompt_k.shape
    rkeys = resp_k.shape[0]
    merged = rows * heads
    flat = lambda a: a.reshape(-1, dim)
    vmem = pl.BlockSpec(memory_space=pltpu.VMEM)
    stats = ((n + 2 + 7) // 8) * 8
    grads = (12, keys // 2, kvh * dim) if n == 4 else (2 * n, keys, kvh * dim)
    results = pl.pallas_call(
        functools.partial(kernel, n, heads, kvh),
        out_shape=[
            jax.ShapeDtypeStruct((merged, dim), BF16),
            jax.ShapeDtypeStruct((merged, dim), BF16),
            jax.ShapeDtypeStruct((rkeys * kvh, dim), BF16),
            jax.ShapeDtypeStruct((rkeys * kvh, dim), BF16),
            jax.ShapeDtypeStruct((keys * kvh, dim), BF16),
            jax.ShapeDtypeStruct((keys * kvh, dim), BF16),
        ],
        in_specs=[pl.BlockSpec(memory_space=pltpu.SMEM)] + [vmem] * 7,
        out_specs=[vmem] * 6,
        scratch_shapes=[
            pltpu.VMEM((n, 2, keys, kvh * dim), BF16),
            pltpu.VMEM((kvh * dim, merged), BF16),
            pltpu.VMEM((kvh * dim, merged), BF16),
            pltpu.VMEM((merged, kvh * dim), BF16),
            pltpu.VMEM((merged, kvh * dim), BF16),
            pltpu.VMEM((n, keys, merged), BF16),
            pltpu.VMEM((rkeys, merged), BF16),
            pltpu.VMEM((keys, merged), BF16),
            pltpu.VMEM((rkeys, merged), F32),
            pltpu.VMEM((dim, merged), F32),
            pltpu.VMEM((dim, merged), F32),
            pltpu.VMEM((stats, merged), F32),
            pltpu.VMEM((stats, merged), F32),
            pltpu.VMEM((8, merged), F32),
            pltpu.VMEM((2, rkeys, kvh * dim), BF16),
            pltpu.VMEM((n + 1, kvh * dim, keys), BF16),
            pltpu.VMEM((keys, kvh * dim), F32),
            pltpu.VMEM((2, keys // 2, kvh * dim), F32),
            pltpu.VMEM(grads, BF16),
            pltpu.VMEM(grads, BF16),
            pltpu.SemaphoreType.DMA((max(12, 2 * n),)),
            pltpu.SemaphoreType.DMA((max(12, 2 * n),)),
            pltpu.SemaphoreType.DMA((grads[0],)),
            pltpu.SemaphoreType.DMA((grads[0],)),
        ],
        compiler_params=pltpu.CompilerParams(
            collective_id=0, has_side_effects=True, vmem_limit_bytes=60 * 1024 * 1024
        ),
        cost_estimate=pl.CostEstimate(
            flops=12 * merged * dim * (n * keys + rkeys),
            bytes_accessed=4 * merged * dim * 2,
            transcendentals=merged * (n * keys + rkeys),
        ),
    )(
        live_rows, flat(resp_q), flat(prompt_k), flat(prompt_v), flat(resp_k), flat(resp_v),
        flat(d_out), segment_ids,
    )
    results = store(results)
    shapes = (resp_q, resp_q, resp_k, resp_v, prompt_k, prompt_v)
    return tuple(r.reshape(s.shape) for r, s in zip(results, shapes))


def solution(mesh):
    split = P(("group", "blk"), "kvh", None)
    return jax.shard_map(
        functools.partial(on_device, mesh.shape["blk"]),
        mesh=mesh,
        in_specs=(split,) * 6 + (P(("group", "blk"), None), P(("group", "blk"))),
        out_specs=(split,) * 6,
        check_vma=False,
    )
```

time: 38.4 us -> 35 us (0.911)
  Pallas kernels: 36.9 us -> 33.5 us
    pallas_call x1, Pallas kernels: 34.5 us -> 31.1 us  [on_device(): pl.pallas_call(functools.partial(kernel, n, heads, kvh), out_shape=[jax.S...]
where the time goes in v3:
time: 35 us; the launch traced here: 34.8 us
  Pallas kernels  33.5 us (96%)
  between operations  1.29 us (4%)
    pallas_call x1, Pallas kernels, on_device(): pl.pallas_call(functools.partial(kernel, n, heads, kvh), out_shape=[jax.S...  31.1 us
    pallas_call x1, Pallas kernels, store(): pl.pallas_call(store_kernel, out_shape=[jax.ShapeDtypeStruct(r.shape, r.d...  2.42 us

profile of v3, /device:TPU:0, one launch (start us, length us, event | category | flops | bytes accessed | tf_op | source)
XLA Modules:
  0.0 34.8 jit_solution(14790951244853499138)
XLA Ops:
  1.3 31.1 %shard_map.127 = (bf16[2048,128]{1,0:T(8,128)(2,1)}, bf16[2048,128]{1,0:T(8,128)(2,1)}, bf16[256,128]{1,0:T(8,128)(2,1)}, bf16[256,128]{1,0:T(8,128)(2,1)}, bf16...) custom-call(s32[1]{0:T(128)S(6)} %copy.14.live_ref, bf16[2048,128]{1,0:T(8,128)(2,1)} %bitcast.12, ...), custom_call_target="tpu_custom_call" | custom-call | flops 3623878656 | bytes 2097152 | tf_op jit(solution)/shard_map/pallas_call | solution.py:375
  32.4 2.4 %shard_map.128 = (bf16[2048,128]{1,0:T(8,128)(2,1)}, bf16[2048,128]{1,0:T(8,128)(2,1)}, bf16[256,128]{1,0:T(8,128)(2,1)}, bf16[256,128]{1,0:T(8,128)(2,1)}, bf16...) custom-call(bf16[2048,128]{1,0:T(8,128)(2,1)} %get-tuple-element.18.refs_0_, bf16[2048,128]{1,0:T(8,128)(2,1)} %get-tuple-element.19.refs_1_, ...), custom_call_target="tpu_custom_call" | custom-call | tf_op jit(solution)/shard_map/pallas_call | solution.py:358
